TPU v7x, 512 devices: a whole 4x4x16 slice. The times are simulated.
512 devices in a mesh: ctx: 64 (over z, x), tp: 8 (over y, core).
Axes of the slice: x: 4, y: 4, z: 16, core: 2. Of those that a mesh axis runs over, the one named last changes fastest.
Arguments:
- tokens: bfloat16 [65536, 4096], P(('ctx', 'tp')), may hold values from -26 to 26
- query_weight: bfloat16 [4096, 2048], P('ctx', 'tp'), may hold values from -0.09375 to 0.09375
- kv_weight: bfloat16 [4096, 2048], P('ctx', 'tp'), may hold values from -0.09375 to 0.09375
- reach: int32 [1024], P('ctx'), may hold values from 1 to 2, as said below
- global_ids: int32 [2], replicated, may hold values from 0 to 1023, as said below
- rand_ids: int32 [1024, 3], replicated, may hold values from -1 to 1023, as said below
Outputs:
- attended: bfloat16 [65536, 2048], P('ctx', 'tp')
Inputs may be any that keep to these rules, and one draw needn't show every extreme that they name: Some query block has reach 2. `global_ids`: distinct block numbers; the last entry is block 1023. `rand_ids`: the -1 entries of a query block come after its other entries; the 16 query blocks of a run (blocks 16 * i to 16 * i + 15) list at most 2 entries, repeats counted, that name blocks of any one run; in some run all entries are filled and some run of key blocks is named by exactly 2 of them.
All inputs are finite; a program needn't handle non-finite values.
Results may differ from a plain program's by a relative error of at most 0.012.
The roundings to bfloat16 on the way count: a program that leaves them out, or rounds other values in their place, can miss the bound.
Values may be sent and summed in bfloat16 or wider, within the bound.
No kernel may reach another device: no remote copies, remote signals or barrier semaphores. Data moves between devices by JAX's collectives and lax.ppermute only.
A program may use at most 64 MiB of HBM per device.

v0:
```python
import jax
import jax.numpy as jnp
from jax import lax
from jax.sharding import PartitionSpec as P

HD = 128
GROUP = 2
BS = 64
WMAX = 2
G = 2
masked_score = -1e30


def with_halo(shard, sides, width):
    for axis, dim in sides:
        size, length = (lax.axis_size(axis), shard.shape[dim])
        up = [(i, (i + 1) % size) for i in range(size - 1)]
        down = [(j, i) for i, j in up]
        last = lax.slice_in_dim(shard, length - width, length, axis=dim)
        initial = lax.slice_in_dim(shard, 0, width, axis=dim)
        before = lax.ppermute(last, axis, up)
        after = lax.ppermute(initial, axis, down)
        shard = jnp.concatenate([before, shard, after], axis=dim)
    return shard


def attend_group(query_group, slab_group, valid_group, kv_local):
    group_blocks = query_group.shape[0]
    slot_count = slab_group.shape[1]
    queries = query_group.reshape(group_blocks, BS, kv_local, GROUP, HD)
    slabs = slab_group.reshape(group_blocks, slot_count, BS, kv_local, 2, HD)
    scores = jnp.einsum(
        "bqkgd,bsjkd->bkgqsj", queries, slabs[:, :, :, :, 0, :], preferred_element_type=jnp.float32
    )
    scores = scores.reshape(scores.shape[:4] + (slot_count * BS,)) * HD ** (-0.5)
    key_live = jnp.repeat(valid_group, BS, axis=1)
    scores = jnp.where(key_live[:, None, None, None, :], scores, masked_score)
    row_max = jnp.max(scores, axis=-1, keepdims=True)
    exponent = jnp.exp(scores - row_max)
    weights = (exponent / jnp.sum(exponent, axis=-1, keepdims=True)).astype(jnp.bfloat16)
    weights = weights.reshape(weights.shape[:4] + (slot_count, BS))
    mixed = jnp.einsum(
        "bkgqsj,bsjkd->bqkgd", weights, slabs[:, :, :, :, 1, :], preferred_element_type=jnp.float32
    )
    return mixed.astype(jnp.bfloat16).reshape(group_blocks * BS, kv_local * GROUP * HD)


def fetch_blocks(key_rows, global_ids, rand_ids, ctx_index, ctx_count):
    row_count, lane_width = key_rows.shape
    run_blocks = row_count // BS
    blocks = key_rows.reshape(run_blocks, BS, lane_width)
    padded = with_halo(key_rows, (("ctx", 0),), WMAX * BS)
    padded_blocks = padded.reshape(run_blocks + 2 * WMAX, BS, lane_width)
    window_kv = jnp.stack(
        [padded_blocks[shift_at : shift_at + run_blocks] for shift_at in range(2 * WMAX + 1)],
        axis=1,
    )
    global_owner = global_ids // run_blocks
    global_local = global_ids % run_blocks
    is_held = (global_owner == ctx_index)[:, None, None]
    sum_term = jnp.where(is_held, blocks[global_local].astype(jnp.float32), 0.0)
    global_kv = lax.psum(sum_term, "ctx").astype(jnp.bfloat16)
    slot_count = run_blocks * rand_ids.shape[1]
    capacity = max(2, (slot_count + ctx_count - 1) // ctx_count)
    listed = rand_ids.reshape(ctx_count, slot_count)
    owners = jnp.where(listed >= 0, listed // run_blocks, -1)
    owned_here = owners == ctx_index
    ranks = jnp.cumsum(owned_here.astype(jnp.int32), axis=1) - 1
    picks = owned_here[:, None, :] & (ranks[:, None, :] == jnp.arange(capacity)[None, :, None])
    local_ids = jnp.sum(jnp.where(picks, listed[:, None, :] % run_blocks, 0), axis=2)
    filled = jnp.any(picks, axis=2)
    outgoing = jnp.where(filled[:, :, None, None], blocks[local_ids], jnp.zeros((), jnp.bfloat16))
    incoming = lax.all_to_all(outgoing, "ctx", split_axis=0, concat_axis=0, tiled=True)
    wanted = lax.dynamic_index_in_dim(owners, ctx_index, 0, keepdims=False)
    slot_order = jnp.arange(slot_count)
    earlier = (wanted[None, :] == wanted[:, None]) & (slot_order[None, :] < slot_order[:, None])
    position = jnp.sum(earlier.astype(jnp.int32), axis=1)
    flat_index = jnp.where(wanted >= 0, wanted * capacity + position, 0)
    random_kv = incoming.reshape(ctx_count * capacity, BS, lane_width)[flat_index]
    random_kv = random_kv.reshape(run_blocks, -1, BS, lane_width)
    return (window_kv, global_kv, random_kv)


def per_device(tokens, query_weight, kv_weight, reach, global_ids, rand_ids):
    ctx_count = lax.axis_size("ctx")
    ctx_index = lax.axis_index("ctx")
    full_query_w, full_kv_w = (
        lax.all_gather(query_weight, "ctx", axis=0, tiled=True),
        lax.all_gather(kv_weight, "ctx", axis=0, tiled=True),
    )
    query_width = full_query_w.shape[1]
    token_piece = lax.all_gather(tokens, "tp", axis=0, tiled=True)
    query_part = jnp.dot(token_piece, full_query_w, preferred_element_type=jnp.float32)
    key_part = jnp.dot(token_piece, full_kv_w, preferred_element_type=jnp.float32)
    projected = jnp.concatenate([query_part, key_part], axis=1)
    query_rows = projected[:, :query_width].astype(jnp.bfloat16)
    key_rows = projected[:, query_width:].astype(jnp.bfloat16)
    window_kv, global_kv, random_kv = fetch_blocks(
        key_rows, global_ids, rand_ids, ctx_index, ctx_count
    )
    row_count, lane_width = key_rows.shape
    run_blocks = row_count // BS
    kv_local = lane_width // (2 * HD)
    offsets = jnp.arange(-WMAX, WMAX + 1)
    first_block = ctx_index * run_blocks
    target = first_block + jnp.arange(run_blocks)[:, None] + offsets[None, :]
    window_live = (
        (jnp.abs(offsets)[None, :] <= reach[:, None])
        & (target >= 0)
        & (target < run_blocks * ctx_count)
    )
    own_lists = lax.dynamic_slice_in_dim(rand_ids, first_block, run_blocks, 0)
    slot_valid = jnp.concatenate(
        [window_live, jnp.ones((run_blocks, G), jnp.bool_), own_lists >= 0], axis=1
    )
    global_tiled = jnp.broadcast_to(global_kv[None], (run_blocks,) + global_kv.shape)
    slab_all = jnp.concatenate([window_kv, global_tiled, random_kv], axis=1)
    slot_total = slab_all.shape[1]
    group_size = max((divisor for divisor in range(1, 9) if run_blocks % divisor == 0))
    group_count = run_blocks // group_size
    query_groups = query_rows.reshape(group_count, group_size, BS, query_width)
    slab_groups = slab_all.reshape(group_count, group_size, slot_total, BS, lane_width)
    valid_groups = slot_valid.reshape(group_count, group_size, slot_total)

    def one_group(operands):
        return attend_group(operands[0], operands[1], operands[2], kv_local)

    outputs = lax.map(one_group, (query_groups, slab_groups, valid_groups))
    return outputs.reshape(row_count, query_width)


def solution(mesh):
    in_specs = (P(("ctx", "tp"), None), P("ctx", "tp"), P("ctx", "tp"), P("ctx"), P(), P())
    out_specs = P("ctx", "tp")
    return jax.shard_map(
        per_device, mesh=mesh, in_specs=in_specs, out_specs=out_specs, check_vma=False
    )
```

profile of v0, /device:TPU:8, one launch (start us, length us, event | category | flops | bytes accessed | tf_op | source)
XLA Modules:
  0.0 769.2 jit_solution(11982867577212984012)
XLA Ops:
  8.0 0.9 copy.68
  10.9 144.8 %all-gather.6.cloned.1.call-done = bf16[4096,256]{1,0:T(8,128)(2,1)} async-done(((bf16[64,256]{1,0:T(8,128)(2,1)}), bf16[4096,256]{1,0:T(8,128)(2,1)}) %all-gather.6.cloned.1.call-update) | async-done | bytes 2097168 | tf_op jit(solution)/shard_map/all_gather | solution.py:89
  155.7 54.8 %all-gather.4.cloned.1.call-done = bf16[1024,4096]{1,0:T(8,128)(2,1)} async-done(((bf16[128,4096]{1,0:T(8,128)(2,1)}), bf16[1024,4096]{1,0:T(8,128)(2,1)}) %all-gather.4.cloned.1.call-update) | async-done | bytes 8388624 | tf_op jit(solution)/shard_map/all_gather | solution.py:92
  210.4 6.3 convolution_convert_fusion.1
  216.8 2.7 gather_fusion.1
  219.5 4.5 broadcast_select_fusion
  224.0 16.0 %all-to-all-start = ((bf16[64,2,64,256]{3,2,1,0:T(8,128)(2,1)}), bf16[64,2,64,256]{3,2,1,0:T(8,128)(2,1)}, u32[]{:S(2)}, u32[]{:S(2)}) async-start(bf16[64,2,64,256]{3,2,1,0:T(8,128)(2,1)} %broadcast_select_fusion), calls=%async_computation | async-start | bytes 8388608 | tf_op jit(solution)/shard_map/all_to_all | solution.py:73
  242.1 1.3 collective-permute-start.1
  243.4 4.5 collective-permute-start
  248.6 184.2 %all-gather.8.cloned.1.call-done = bf16[4096,256]{1,0:T(8,128)(2,1)} async-done(((bf16[64,256]{1,0:T(8,128)(2,1)}), bf16[4096,256]{1,0:T(8,128)(2,1)}) %all-gather.8.cloned.1.call-update) | async-done | bytes 2097168 | tf_op jit(solution)/shard_map/all_gather | solution.py:88
  432.9 6.3 convolution_convert_fusion
  439.2 279.7 %all-reduce.1 = bf16[2,64,256]{2,1,0:T(8,128)(2,1)S(1)} all-reduce(f32[2,64,256]{2,1,0:T(8,128)S(1)} %convert_select_fusion), channel_id=1, replica_groups=mesh['ctx'=64,'tp'=8] {'ctx'}, use_global_device_ids=true, to_apply=%region_0.1 | all-reduce | flops 32768 | bytes 196608 | tf_op jit(solution)/shard_map/psum | solution.py:62
  719.1 0.9 constant_dynamic-update-slice_fusion.6
  720.0 0.9 constant_dynamic-update-slice_fusion.5
  720.8 0.9 constant_dynamic-update-slice_fusion.4
  721.7 0.9 constant_dynamic-update-slice_fusion.3
  723.4 1.1 broadcast_dynamic-update-slice_fusion
  724.5 2.8 gather_fusion.2
  727.4 1.3 constant_dynamic-update-slice_fusion.1
  728.7 34.0 %while.10 = (s32[]{:T(128)}, bf16[2,512,256]{2,1,0:T(8,128)(2,1)}, bf16[2,8,10,64,256]{4,3,2,1,0:T(8,128)(2,1)}, pred[2,8,10]{2,1,0:T(8,128)(4,1)S(1)}, bf16[2,8,64,256]{3,2,1,0:T(8,128)(2,1)S(1)}, /*index=5*/s32[]{:T(128)}) while((s32[]{:T(128)}, bf16[2,512,256]{2,1,0:T(8,128)(2,1)}, bf16[2,8,10,64,256]{4,3,2,1,0:T(8,128)(2,1)}, ...), condition=%wide.region_8.9_spmd, body=%wide.region_5.8_spmd.sunk | while | flops 343537664 | bytes 33575460 | solution.py:128
  728.8 3.6 constant_dynamic-slice_fusion.6
  732.3 3.5 reshape.320
  735.9 3.7 fusion.55
  739.6 1.3 bitcast_reduce_fusion.2
  740.9 1.5 fusion.56
  742.4 1.9 fusion.57
  745.7 3.6 constant_dynamic-slice_fusion.6
  749.3 3.5 reshape.320
  752.9 3.7 fusion.55
  756.6 1.3 bitcast_reduce_fusion.2
  757.9 1.5 fusion.56
  759.4 1.9 fusion.57
  (68 shorter events, 9.7 us)
Async XLA Ops:
  6.5 149.1 %all-gather.6.cloned.1.call-start = ((), (), s32[]{:S(2)}) async-start(), calls=%async_computation.2 | async-start | bytes 2129920 | tf_op jit(solution)/shard_map/all_gather | solution.py:89
  7.3 203.2 %all-gather.4.cloned.1.call-start = ((), (), s32[]{:S(2)}) async-start(), calls=%async_computation.1 | async-start | bytes 9437184 | tf_op jit(solution)/shard_map/all_gather | solution.py:92
  224.0 17.6 %copy-start = (s32[16]{0:T(128)S(1)}, s32[16]{0:T(128)}, u32[]{:S(2)}) copy-start(s32[16]{0:T(128)} %param.11) | copy-start | bytes 196
  224.0 18.1 %copy-start.3 = (s32[2]{0:T(128)S(1)}, s32[2]{0:T(128)}, u32[]{:S(2)}) copy-start(s32[2]{0:T(128)} %param.12) | copy-start | bytes 28
  224.0 500.5 %all-to-all-start = ((bf16[64,2,64,256]{3,2,1,0:T(8,128)(2,1)}), bf16[64,2,64,256]{3,2,1,0:T(8,128)(2,1)}, u32[]{:S(2)}, u32[]{:S(2)}) async-start(bf16[64,2,64,256]{3,2,1,0:T(8,128)(2,1)} %broadcast_select_fusion), calls=%async_computation | async-start | bytes 8388608 | tf_op jit(solution)/shard_map/all_to_all | solution.py:73
  240.0 192.9 %all-gather.8.cloned.1.call-start = ((), (), s32[]{:S(2)}) async-start(), calls=%async_computation.3 | async-start | bytes 2129920 | tf_op jit(solution)/shard_map/all_gather | solution.py:88
  242.1 476.8 %collective-permute-start.1 = (bf16[128,256]{1,0:T(8,128)(2,1)S(1)}, bf16[128,256]{1,0:T(8,128)(2,1)S(1)}, u32[]{:S(2)}, u32[]{:S(2)}) collective-permute-start(bf16[128,256]{1,0:T(8,128)(2,1)S(1)} %get-tuple-element.61), channel_id=1, source_target_pairs={{8,0},{16,8},{24,16},{32,24},{40,32},{48,40},{56,48},{64,56},{72,6... | collective-permute-start | bytes 196616 | tf_op jit(solution)/shard_map/ppermute | solution.py:22
  243.4 475.5 %collective-permute-start = (bf16[128,256]{1,0:T(8,128)(2,1)S(1)}, bf16[128,256]{1,0:T(8,128)(2,1)S(1)}, u32[]{:S(2)}, u32[]{:S(2)}) collective-permute-start(bf16[128,256]{1,0:T(8,128)(2,1)S(1)} %get-tuple-element.62), channel_id=1, source_target_pairs={{0,8},{8,16},{16,24},{24,32},{32,40},{40,48},{48,56},{56,64},{64,7... | collective-permute-start | bytes 196616 | tf_op jit(solution)/shard_map/ppermute | solution.py:21
  742.4 2.4 copy-start.1
  744.9 0.8 copy-start.2
  759.4 2.4 copy-start.1
  761.8 0.8 copy-start.2
Sparse Core Ops, SparseCore 0:
  10.3 145.3 all-gather.5
  157.8 52.5 all-gather.3
  243.8 189.0 all-gather.7
where the time goes:
time: 770 us; the launch traced here: 769 us
  waiting for transfers between devices  386 us (50%)
  blocking collectives  280 us (36%)
  local copies, waits for them, and re-layouts  39.2 us (5%)
  starting transfers between devices  21.9 us (3%)
  matrix products  19 us (2%)
  between operations  13.3 us (2%)
  other arithmetic  9.89 us (1%)
    psum x1, blocking collectives, fetch_blocks(): global_kv = lax.psum(sum_term, 'ctx').astype(jnp.bfloat16)  280 us
    all_gather x1, waiting for transfers between devices, per_device(): lax.all_gather(query_weight, 'ctx', axis=0, tiled=True)  184 us
    all_gather x1, waiting for transfers between devices, per_device(): lax.all_gather(kv_weight, 'ctx', axis=0, tiled=True)  145 us
    all_gather x1, waiting for transfers between devices, per_device(): token_piece = lax.all_gather(tokens, 'tp', axis=0, tiled=True)  54.8 us
    all_to_all x1, starting transfers between devices, fetch_blocks(): lax.all_to_all(outgoing, 'ctx', split_axis=0, concat_axis=0, tiled=True)  16 us
  transfers between devices with their start and end apart: 6, of which 3 were waited for; matrix products, arithmetic and copies ran while one was open for 2% of the time, Pallas kernels for 0%

commit v1 on v0

--- a/solution.py
+++ b/solution.py
@@ -59,7 +59,7 @@
     global_local = global_ids % run_blocks
     is_held = (global_owner == ctx_index)[:, None, None]
     sum_term = jnp.where(is_held, blocks[global_local].astype(jnp.float32), 0.0)
-    global_kv = lax.psum(sum_term, "ctx").astype(jnp.bfloat16)
+    global_kv = jnp.sum(lax.all_gather(sum_term, "ctx"), axis=0).astype(jnp.bfloat16)
     slot_count = run_blocks * rand_ids.shape[1]
     capacity = max(2, (slot_count + ctx_count - 1) // ctx_count)
     listed = rand_ids.reshape(ctx_count, slot_count)

time: 770 us -> 614 us (0.80)
  the two profiles are of different devices: /device:TPU:8 before, /device:TPU:32 now
where the time goes in v1:
time: 614 us; the launch traced here: 613 us
  waiting for transfers between devices  504 us (82%)
  local copies, waits for them, and re-layouts  39.3 us (6%)
  starting transfers between devices  22.8 us (4%)
  matrix products  19 us (3%)
  other arithmetic  15.1 us (2%)
  between operations  13.3 us (2%)
    all_gather x1, waiting for transfers between devices, per_device(): lax.all_gather(query_weight, 'ctx', axis=0, tiled=True)  152 us
    all_gather x1, waiting for transfers between devices, per_device(): lax.all_gather(kv_weight, 'ctx', axis=0, tiled=True)  143 us
    all_gather x1, waiting for transfers between devices, fetch_blocks(): lax.all_gather(sum_term, 'ctx')  119 us
    all_gather x1, waiting for transfers between devices, per_device(): token_piece = lax.all_gather(tokens, 'tp', axis=0, tiled=True)  55.7 us
    ppermute x1, waiting for transfers between devices, with_halo(): after = lax.ppermute(initial, axis, down)  28.1 us
    all_to_all x1, starting transfers between devices, fetch_blocks(): lax.all_to_all(outgoing, 'ctx', split_axis=0, concat_axis=0, tiled=True)  15.9 us
  transfers between devices with their start and end apart: 7, of which 7 were waited for; matrix products, arithmetic and copies ran while one was open for 5% of the time, Pallas kernels for 0%

profile of v1, /device:TPU:32, one launch (start us, length us, event | category | flops | bytes accessed | tf_op | source)
XLA Modules:
  0.0 613.3 jit_solution(18011057917492657366)
XLA Ops:
  8.7 0.9 copy.81
  12.3 143.1 %all-gather.7.cloned.1.call-done = bf16[4096,256]{1,0:T(8,128)(2,1)} async-done(((bf16[64,256]{1,0:T(8,128)(2,1)}), bf16[4096,256]{1,0:T(8,128)(2,1)}) %all-gather.7.cloned.1.call-update) | async-done | bytes 2097168 | tf_op jit(solution)/shard_map/all_gather | solution.py:89
  155.3 55.7 %all-gather.5.cloned.1.call-done = bf16[1024,4096]{1,0:T(8,128)(2,1)} async-done(((bf16[128,4096]{1,0:T(8,128)(2,1)}), bf16[1024,4096]{1,0:T(8,128)(2,1)}) %all-gather.5.cloned.1.call-update) | async-done | bytes 8388624 | tf_op jit(solution)/shard_map/all_gather | solution.py:92
  211.0 6.3 %convolution_convert_fusion.1 = bf16[1024,256]{1,0:T(8,128)(2,1)S(1)} fusion(bf16[1024,4096]{1,0:T(8,128)(2,1)} %all-gather.5.cloned.1.call-done, bf16[4096,256]{1,0:T(8,128)(2,1)} %all-gather.7.cloned.1.call-done), kind=kOutput, calls=%fused_computation.28 | convolution fusion | flops 2147745792 | bytes 11010048 | tf_op jit(solution)/shard_map/dot_general | solution.py:94
  217.9 2.8 gather_fusion.1
  220.6 4.5 broadcast_select_fusion
  225.1 15.9 %all-to-all-start = ((bf16[64,2,64,256]{3,2,1,0:T(8,128)(2,1)}), bf16[64,2,64,256]{3,2,1,0:T(8,128)(2,1)}, u32[]{:S(2)}, u32[]{:S(2)}) async-start(bf16[64,2,64,256]{3,2,1,0:T(8,128)(2,1)} %broadcast_select_fusion), calls=%async_computation | async-start | bytes 8388608 | tf_op jit(solution)/shard_map/all_to_all | solution.py:73
  243.2 4.6 collective-permute-start.1
  247.8 2.1 collective-permute-start
  249.9 151.9 %all-gather.11.cloned.1.call-done = bf16[4096,256]{1,0:T(8,128)(2,1)} async-done(((bf16[64,256]{1,0:T(8,128)(2,1)}), bf16[4096,256]{1,0:T(8,128)(2,1)}) %all-gather.11.cloned.1.call-update) | async-done | bytes 2097168 | tf_op jit(solution)/shard_map/all_gather | solution.py:88
  401.8 6.3 %convolution_convert_fusion = bf16[1024,256]{1,0:T(8,128)(2,1)S(1)} fusion(bf16[1024,4096]{1,0:T(8,128)(2,1)} %all-gather.5.cloned.1.call-done, bf16[4096,256]{1,0:T(8,128)(2,1)} %all-gather.11.cloned.1.call-done), kind=kOutput, calls=%fused_computation.27 | convolution fusion | flops 2147745792 | bytes 11010048 | tf_op jit(solution)/shard_map/dot_general | solution.py:93
  408.1 28.1 %collective-permute-done.1 = bf16[128,256]{1,0:T(8,128)(2,1)S(1)} collective-permute-done((bf16[128,256]{1,0:T(8,128)(2,1)S(1)}, bf16[128,256]{1,0:T(8,128)(2,1)S(1)}, u32[]{:S(2)}, u32[]{:S(2)}) %collective-permute-start.1) | collective-permute-done | bytes 65568 | tf_op jit(solution)/shard_map/ppermute | solution.py:22
  436.2 1.5 collective-permute-done
  442.1 2.7 all-to-all-done
  444.8 2.9 gather_fusion.2
  447.7 118.8 %all-gather.9.cloned.1.call-done = f32[64,2,64,256]{3,2,1,0:T(8,128)} async-done(((f32[1,2,64,256]{3,2,1,0:T(8,128)}), f32[64,2,64,256]{3,2,1,0:T(8,128)}) %all-gather.9.cloned.1.call-update) | async-done | bytes 8388624 | tf_op jit(solution)/shard_map/all_gather | solution.py:62
  566.4 3.9 reduce_sum.40
  570.4 1.1 broadcast_dynamic-update-slice_fusion
  571.5 1.3 constant_dynamic-update-slice_fusion.1
  572.7 34.0 %while.10 = (s32[]{:T(128)}, bf16[2,512,256]{2,1,0:T(8,128)(2,1)}, bf16[2,8,10,64,256]{4,3,2,1,0:T(8,128)(2,1)}, pred[2,8,10]{2,1,0:T(8,128)(4,1)S(1)}, bf16[2,8,64,256]{3,2,1,0:T(8,128)(2,1)S(1)}, /*index=5*/s32[]{:T(128)}) while((s32[]{:T(128)}, bf16[2,512,256]{2,1,0:T(8,128)(2,1)}, bf16[2,8,10,64,256]{4,3,2,1,0:T(8,128)(2,1)}, ...), condition=%wide.region_8.9_spmd, body=%wide.region_5.8_spmd.sunk | while | flops 343537664 | bytes 33575460 | solution.py:128
  572.8 3.6 constant_dynamic-slice_fusion.6
  576.4 3.5 reshape.335
  580.0 3.7 fusion.55
  583.7 1.3 bitcast_reduce_fusion.2
  585.0 1.5 fusion.56
  586.5 1.9 fusion.57
  589.8 3.6 constant_dynamic-slice_fusion.6
  593.4 3.5 reshape.335
  597.0 3.7 fusion.55
  600.7 1.3 bitcast_reduce_fusion.2
  602.0 1.5 fusion.56
  603.5 1.9 fusion.57
  (69 shorter events, 14.5 us)
Async XLA Ops:
  6.5 148.8 %all-gather.7.cloned.1.call-start = ((), (), s32[]{:S(2)}) async-start(), calls=%async_computation.2 | async-start | bytes 2129920 | tf_op jit(solution)/shard_map/all_gather | solution.py:89
  7.3 203.7 %all-gather.5.cloned.1.call-start = ((), (), s32[]{:S(2)}) async-start(), calls=%async_computation.1 | async-start | bytes 9437184 | tf_op jit(solution)/shard_map/all_gather | solution.py:92
  8.0 393.8 %all-gather.11.cloned.1.call-start = ((), (), s32[]{:S(2)}) async-start(), calls=%async_computation.4 | async-start | bytes 2129920 | tf_op jit(solution)/shard_map/all_gather | solution.py:88
  225.1 17.6 %copy-start = (s32[16]{0:T(128)S(1)}, s32[16]{0:T(128)}, u32[]{:S(2)}) copy-start(s32[16]{0:T(128)} %param.11) | copy-start | bytes 196
  225.1 219.7 %all-to-all-start = ((bf16[64,2,64,256]{3,2,1,0:T(8,128)(2,1)}), bf16[64,2,64,256]{3,2,1,0:T(8,128)(2,1)}, u32[]{:S(2)}, u32[]{:S(2)}) async-start(bf16[64,2,64,256]{3,2,1,0:T(8,128)(2,1)} %broadcast_select_fusion), calls=%async_computation | async-start | bytes 8388608 | tf_op jit(solution)/shard_map/all_to_all | solution.py:73
  241.1 325.4 %all-gather.9.cloned.1.call-start = ((), (), s32[]{:S(2)}) async-start(), calls=%async_computation.3 | async-start | bytes 8519680 | tf_op jit(solution)/shard_map/all_gather | solution.py:62
  243.2 193.0 %collective-permute-start.1 = (bf16[128,256]{1,0:T(8,128)(2,1)S(1)}, bf16[128,256]{1,0:T(8,128)(2,1)S(1)}, u32[]{:S(2)}, u32[]{:S(2)}) collective-permute-start(bf16[128,256]{1,0:T(8,128)(2,1)S(1)} %get-tuple-element.61), channel_id=1, source_target_pairs={{8,0},{16,8},{24,16},{32,24},{40,32},{48,40},{56,48},{64,56},{72,6... | collective-permute-start | bytes 196616 | tf_op jit(solution)/shard_map/ppermute | solution.py:22
  247.8 189.9 %collective-permute-start = (bf16[128,256]{1,0:T(8,128)(2,1)S(1)}, bf16[128,256]{1,0:T(8,128)(2,1)S(1)}, u32[]{:S(2)}, u32[]{:S(2)}) collective-permute-start(bf16[128,256]{1,0:T(8,128)(2,1)S(1)} %get-tuple-element.62), channel_id=1, source_target_pairs={{0,8},{8,16},{16,24},{24,32},{32,40},{40,48},{48,56},{56,64},{64,7... | collective-permute-start | bytes 196616 | tf_op jit(solution)/shard_map/ppermute | solution.py:21
  586.5 2.4 copy-start.1
  588.9 0.8 copy-start.2
  603.5 2.4 copy-start.1
  606.0 0.8 copy-start.2
Sparse Core Ops, SparseCore 0:
  10.3 144.9 all-gather.6
  157.5 53.4 all-gather.4
  213.9 187.8 all-gather.10
  404.6 161.8 all-gather.8
